TPU v7x, 32 devices: a whole 2x2x4 slice. The times are simulated.
32 devices in a mesh: index: 16 (over z, y, x), query: 2 (over core).
Axes of the slice: x: 2, y: 2, z: 4, core: 2. Of those that a mesh axis runs over, the one named last changes fastest.
Arguments:
- queries: bfloat16 [64, 32, 128], P('query'), may hold values from -6 to 6
- passages: bfloat16 [2048, 128, 128], P(('index', 'query')), may hold values from -0.5 to 0.5
- lengths: int32 [2048], P(('index', 'query')), may hold values from 1 to 128
- candidates: int32 [64, 256], P('query', 'index'), may hold values from 0 to 2047, as said below
Outputs:
- scores: float32 [64, 256], P('query', 'index')
Inputs may be any that keep to these rules, and one draw needn't show every extreme that they name: Block b is stored on the device of flat position b // 64 along index+query. The 32 x 16 candidates held by one device name blocks of any one storing device at most 32 times, and exactly 32 times for some storing device.
All inputs are finite; a program needn't handle non-finite values.
Results may differ from a plain program's by a relative error of at most 0.0003.
Values may be sent and summed in bfloat16 or wider, within the bound.
A program may use at most 64 MiB of HBM per device.

v0:
```python
import math

import jax
import jax.numpy as jnp
from jax import lax
from jax.sharding import PartitionSpec as P


def score_slots(slot_rows, slot_blocks, passages, lengths):
    slot_total = slot_blocks.shape[0]
    group = math.gcd(slot_total, 128)
    token_count = passages.shape[1]

    def score_group(packed):
        query_rows, block_ids = packed
        safe_ids = jnp.maximum(block_ids, 0)
        block_rows = passages[safe_ids]
        similar = jnp.einsum(
            "gtd,gpd->gtp", query_rows, block_rows, preferred_element_type=jnp.float32
        )
        token_pos = lax.broadcasted_iota(jnp.int32, (1, 1, token_count), 2)
        live = token_pos < lengths[safe_ids][:, None, None]
        best = jnp.max(jnp.where(live, similar, -jnp.inf), axis=2)
        return jnp.where(block_ids >= 0, jnp.mean(best, axis=1), jnp.float32(0.0))

    grouped_rows = slot_rows.reshape((slot_total // group, group) + slot_rows.shape[1:])
    grouped_ids = slot_blocks.reshape(slot_total // group, group)
    results = lax.map(score_group, (grouped_rows, grouped_ids))
    return results.reshape(slot_total)


def shards(queries, passages, lengths, candidates):
    n_index = lax.axis_size("index")
    n_query = lax.axis_size("query")
    devices = n_index * n_query
    q_local, cand_local = candidates.shape
    blk_local = passages.shape[0]
    request_count = q_local * cand_local
    capacity = max(2, 2 * request_count // devices)
    slot_total = devices * capacity
    flat_ids = candidates.reshape(request_count)
    owner = flat_ids // blk_local
    position = jnp.arange(request_count, dtype=jnp.int32)
    earlier = (owner[None, :] == owner[:, None]) & (position[None, :] < position[:, None])
    owner_rank = jnp.sum(earlier, axis=1)
    target = owner * capacity + owner_rank
    slot_request = jnp.full((slot_total,), -1, jnp.int32).at[target].set(position)
    slot_used = slot_request >= 0
    safe_request = jnp.maximum(slot_request, 0)
    slot_block = jnp.where(slot_used, flat_ids[safe_request] % blk_local, -1)
    slot_query = jnp.where(slot_used, safe_request // cand_local, 0)
    grid_shape = (n_index, n_query, capacity)
    sent_rows = queries[slot_query].reshape(grid_shape + queries.shape[1:])
    got_rows, got_blocks = (
        lax.all_to_all(
            lax.all_to_all(sent_rows, "index", split_axis=0, concat_axis=0, tiled=True),
            "query",
            split_axis=1,
            concat_axis=1,
            tiled=True,
        ),
        lax.all_to_all(
            lax.all_to_all(
                slot_block.reshape(grid_shape), "index", split_axis=0, concat_axis=0, tiled=True
            ),
            "query",
            split_axis=1,
            concat_axis=1,
            tiled=True,
        ),
    )
    got_rows = got_rows.reshape((slot_total,) + queries.shape[1:])
    results = score_slots(got_rows, got_blocks.reshape(slot_total), passages, lengths)
    returned = lax.all_to_all(
        lax.all_to_all(
            results.reshape(grid_shape), "index", split_axis=0, concat_axis=0, tiled=True
        ),
        "query",
        split_axis=1,
        concat_axis=1,
        tiled=True,
    )
    return returned.reshape(slot_total)[target].reshape(q_local, cand_local)


def solution(mesh):
    in_specs = (
        P("query", None, None),
        P(("index", "query"), None, None),
        P(("index", "query")),
        P("query", "index"),
    )
    out_specs = P("query", "index")
    return jax.shard_map(shards, mesh=mesh, in_specs=in_specs, out_specs=out_specs, check_vma=False)
```

profile of v0, /device:TPU:1, one launch (start us, length us, event | category | flops | bytes accessed | tf_op | source)
XLA Modules:
  0.0 365.4 jit_solution(9064946191604811967)
XLA Ops:
  0.0 0.8 copy.30
  1.0 0.2 convert_reduce_fusion
  1.3 2.4 scatter_custom_fusion
  3.8 6.9 %gather_fusion.2 = s32[1024]{0:T(1024)S(1)} fusion(s32[512]{0:T(512)S(1)} %reshape.186, s32[1024]{0:T(1024)S(1)} %get-tuple-element.51), kind=kCustom, calls=%fused_computation.2 | custom fusion | bytes 12288 | tf_op jit(solution)/shard_map/gather | solution.py:50
  10.6 0.7 reshape.187
  11.3 7.4 %all-to-all-start = ((s32[16,2,32]{2,1,0:T(2,128)}), s32[16,2,32]{2,1,0:T(2,128)S(1)}, u32[]{:S(2)}, u32[]{:S(2)}) async-start(s32[16,2,32]{2,1,0:T(2,128)} %reshape.187), calls=%async_computation | async-start | bytes 32768 | tf_op jit(solution)/shard_map/all_to_all | solution.py:63
  18.8 9.9 %gather_fusion.3 = bf16[1024,32,128]{2,1,0:T(8,128)(2,1)} fusion(bf16[32,32,128]{2,1,0:T(8,128)(2,1)S(1)} %copy-done, s32[1024]{0:T(1024)S(1)} %get-tuple-element.50), kind=kCustom, calls=%fused_computation.3 | custom fusion | bytes 16781312 | tf_op jit(solution)/shard_map/gather | solution.py:53
  28.8 4.3 %all_to_all.30 = s32[2,1,512]{2,1,0:T(1,128)S(1)} all-to-all(s32[2,1,512]{2,1,0:T(1,128)S(1)} %reshape.245), channel_id=1, replica_groups=mesh['index'=16,'query'=2] {'query'}, dimensions={0} | all-to-all | bytes 8192 | tf_op jit(solution)/shard_map/all_to_all | solution.py:62
  33.1 6.7 %all-to-all-start.2 = ((bf16[16,2,32,32,128]{4,3,2,1,0:T(8,128)(2,1)}), bf16[16,2,32,32,128]{4,3,2,1,0:T(8,128)(2,1)}, u32[]{:S(2)}, u32[]{:S(2)}) async-start(bf16[16,2,32,32,128]{4,3,2,1,0:T(8,128)(2,1)} %bitcast.28), calls=%async_computation.2 | async-start | bytes 16777216 | tf_op jit(solution)/shard_map/all_to_all | solution.py:56
  39.7 0.5 broadcast.214
  40.3 0.6 reduce
  41.0 155.9 %all-to-all-done.2 = bf16[16,2,32,32,128]{4,3,2,1,0:T(8,128)(2,1)} async-done(((bf16[16,2,32,32,128]{4,3,2,1,0:T(8,128)(2,1)}), bf16[16,2,32,32,128]{4,3,2,1,0:T(8,128)(2,1)}, u32[]{:S(2)}, u32[]{:S(2)}) %all-to-all-start.2) | async-done | bytes 8388640 | tf_op jit(solution)/shard_map/all_to_all | solution.py:56
  196.9 8.9 %copy.34 = bf16[16,2,32,32,128]{4,3,2,0,1:T(8,128)(2,1)} copy(bf16[16,2,32,32,128]{4,3,2,1,0:T(8,128)(2,1)} %all-to-all-done.2) | data formatting | bytes 16777216 | tf_op jit(solution)/shard_map/all_to_all | solution.py:56
  205.8 20.5 %all_to_all.31 = bf16[16,2,32,32,128]{4,3,2,0,1:T(8,128)(2,1)} all-to-all(bf16[16,2,32,32,128]{4,3,2,0,1:T(8,128)(2,1)} %copy.34), channel_id=1, replica_groups=mesh['index'=16,'query'=2] {'query'}, dimensions={1} | all-to-all | bytes 16777216 | tf_op jit(solution)/shard_map/all_to_all | solution.py:55
  226.3 9.1 %copy.35 = bf16[16,2,32,32,128]{4,3,2,1,0:T(8,128)(2,1)} copy(bf16[16,2,32,32,128]{4,3,2,0,1:T(8,128)(2,1)} %all_to_all.31) | data formatting | bytes 16777216 | tf_op jit(solution)/shard_map/all_to_all | solution.py:55
  235.4 75.9 %while.10 = (s32[]{:T(128)}, f32[8,128]{1,0:T(8,128)S(1)}, s32[8,128]{1,0:T(8,128)S(1)}, s32[64]{0:T(128)S(1)}, bf16[8,128,32,128]{3,2,1,0:T(8,128)(2,1)}, /*ind...) while((s32[]{:T(128)}, f32[8,128]{1,0:T(8,128)S(1)}, s32[8,128]{1,0:T(8,128)S(1)}, ...), condition=%wide.region_5.6_spmd, body=%wide.region_2.5_spmd.sunk | while | flops 135284096 | bytes 13708909 | solution.py:28
  235.5 3.1 gather_fusion
  238.5 1.2 gather_fusion.1
  239.8 4.9 %select_reduce_fusion.2 = f32[128,32]{1,0:T(8,128)S(1)} fusion(bf16[128,128,128]{2,1,0:T(8,128)(2,1)} %gather_fusion, bf16[8,128,32,128]{3,2,1,0:T(8,128)(2,1)} %get-tuple-element.111, s32[]{:T(128)} %get-tuple-element.98, pred[128,128]{1,0:T(8,128)(4,1)S(1)} %iota_compare_fusion.3), kind=kOutput, calls=%fused_computation.6.clone.1 | convolution fusion | flops 135262208 | bytes 5276160 | tf_op jit(solution)/shard_map/while/body/eval_jaxpr/gtd,gpd->gtp/dot_general | solution.py:18
  244.9 3.1 gather_fusion
  248.0 1.2 gather_fusion.1
  249.3 4.9 %select_reduce_fusion.2 = f32[128,32]{1,0:T(8,128)S(1)} fusion(bf16[128,128,128]{2,1,0:T(8,128)(2,1)} %gather_fusion, bf16[8,128,32,128]{3,2,1,0:T(8,128)(2,1)} %get-tuple-element.111, s32[]{:T(128)} %get-tuple-element.98, pred[128,128]{1,0:T(8,128)(4,1)S(1)} %iota_compare_fusion.3), kind=kOutput, calls=%fused_computation.6.clone.1 | convolution fusion | flops 135262208 | bytes 5276160 | tf_op jit(solution)/shard_map/while/body/eval_jaxpr/gtd,gpd->gtp/dot_general | solution.py:18
  254.4 3.1 gather_fusion
  257.5 1.2 gather_fusion.1
  258.8 4.9 %select_reduce_fusion.2 = f32[128,32]{1,0:T(8,128)S(1)} fusion(bf16[128,128,128]{2,1,0:T(8,128)(2,1)} %gather_fusion, bf16[8,128,32,128]{3,2,1,0:T(8,128)(2,1)} %get-tuple-element.111, s32[]{:T(128)} %get-tuple-element.98, pred[128,128]{1,0:T(8,128)(4,1)S(1)} %iota_compare_fusion.3), kind=kOutput, calls=%fused_computation.6.clone.1 | convolution fusion | flops 135262208 | bytes 5276160 | tf_op jit(solution)/shard_map/while/body/eval_jaxpr/gtd,gpd->gtp/dot_general | solution.py:18
  263.9 3.1 gather_fusion
  267.0 1.2 gather_fusion.1
  268.3 4.9 %select_reduce_fusion.2 = f32[128,32]{1,0:T(8,128)S(1)} fusion(bf16[128,128,128]{2,1,0:T(8,128)(2,1)} %gather_fusion, bf16[8,128,32,128]{3,2,1,0:T(8,128)(2,1)} %get-tuple-element.111, s32[]{:T(128)} %get-tuple-element.98, pred[128,128]{1,0:T(8,128)(4,1)S(1)} %iota_compare_fusion.3), kind=kOutput, calls=%fused_computation.6.clone.1 | convolution fusion | flops 135262208 | bytes 5276160 | tf_op jit(solution)/shard_map/while/body/eval_jaxpr/gtd,gpd->gtp/dot_general | solution.py:18
  273.4 3.1 gather_fusion
  276.5 1.2 gather_fusion.1
  277.8 4.9 %select_reduce_fusion.2 = f32[128,32]{1,0:T(8,128)S(1)} fusion(bf16[128,128,128]{2,1,0:T(8,128)(2,1)} %gather_fusion, bf16[8,128,32,128]{3,2,1,0:T(8,128)(2,1)} %get-tuple-element.111, s32[]{:T(128)} %get-tuple-element.98, pred[128,128]{1,0:T(8,128)(4,1)S(1)} %iota_compare_fusion.3), kind=kOutput, calls=%fused_computation.6.clone.1 | convolution fusion | flops 135262208 | bytes 5276160 | tf_op jit(solution)/shard_map/while/body/eval_jaxpr/gtd,gpd->gtp/dot_general | solution.py:18
  282.9 3.1 gather_fusion
  286.0 1.2 gather_fusion.1
  287.3 4.9 %select_reduce_fusion.2 = f32[128,32]{1,0:T(8,128)S(1)} fusion(bf16[128,128,128]{2,1,0:T(8,128)(2,1)} %gather_fusion, bf16[8,128,32,128]{3,2,1,0:T(8,128)(2,1)} %get-tuple-element.111, s32[]{:T(128)} %get-tuple-element.98, pred[128,128]{1,0:T(8,128)(4,1)S(1)} %iota_compare_fusion.3), kind=kOutput, calls=%fused_computation.6.clone.1 | convolution fusion | flops 135262208 | bytes 5276160 | tf_op jit(solution)/shard_map/while/body/eval_jaxpr/gtd,gpd->gtp/dot_general | solution.py:18
  292.4 3.1 gather_fusion
  295.4 1.2 gather_fusion.1
  296.8 4.9 %select_reduce_fusion.2 = f32[128,32]{1,0:T(8,128)S(1)} fusion(bf16[128,128,128]{2,1,0:T(8,128)(2,1)} %gather_fusion, bf16[8,128,32,128]{3,2,1,0:T(8,128)(2,1)} %get-tuple-element.111, s32[]{:T(128)} %get-tuple-element.98, pred[128,128]{1,0:T(8,128)(4,1)S(1)} %iota_compare_fusion.3), kind=kOutput, calls=%fused_computation.6.clone.1 | convolution fusion | flops 135262208 | bytes 5276160 | tf_op jit(solution)/shard_map/while/body/eval_jaxpr/gtd,gpd->gtp/dot_general | solution.py:18
  301.9 3.1 gather_fusion
  304.9 1.2 gather_fusion.1
  306.3 4.9 %select_reduce_fusion.2 = f32[128,32]{1,0:T(8,128)S(1)} fusion(bf16[128,128,128]{2,1,0:T(8,128)(2,1)} %gather_fusion, bf16[8,128,32,128]{3,2,1,0:T(8,128)(2,1)} %get-tuple-element.111, s32[]{:T(128)} %get-tuple-element.98, pred[128,128]{1,0:T(8,128)(4,1)S(1)} %iota_compare_fusion.3), kind=kOutput, calls=%fused_computation.6.clone.1 | convolution fusion | flops 135262208 | bytes 5276160 | tf_op jit(solution)/shard_map/while/body/eval_jaxpr/gtd,gpd->gtp/dot_general | solution.py:18
  311.3 0.7 reshape_reshape.11
  312.0 37.5 %all-to-all-start.4 = ((f32[16,2,32]{2,1,0:T(2,128)}), f32[16,2,32]{2,1,0:T(2,128)S(1)}, u32[]{:S(2)}, u32[]{:S(2)}) async-start(f32[16,2,32]{2,1,0:T(2,128)} %reshape_reshape.11), calls=%async_computation.4 | async-start | bytes 32768 | tf_op jit(solution)/shard_map/all_to_all | solution.py:75
  349.5 6.2 %all-to-all-done.4 = f32[16,2,32]{2,1,0:T(2,128)S(1)} async-done(((f32[16,2,32]{2,1,0:T(2,128)}), f32[16,2,32]{2,1,0:T(2,128)S(1)}, u32[]{:S(2)}, u32[]{:S(2)}) %all-to-all-start.4) | async-done | bytes 4128 | tf_op jit(solution)/shard_map/all_to_all | solution.py:75
  355.8 5.1 %all_to_all.32 = f32[2,1,512]{2,1,0:T(1,128)S(1)} all-to-all(f32[2,1,512]{2,1,0:T(1,128)S(1)} %reshape.247), channel_id=1, replica_groups=mesh['index'=16,'query'=2] {'query'}, dimensions={0} | all-to-all | bytes 8192 | tf_op jit(solution)/shard_map/all_to_all | solution.py:74
  360.9 0.5 broadcast.215
  361.5 0.7 reduce.1
  362.3 2.3 gather_fusion.4
  364.7 0.7 copy.38
  (75 shorter events, 2.9 us)
Async XLA Ops:
  0.0 18.7 %copy-start = (bf16[32,32,128]{2,1,0:T(8,128)(2,1)S(1)}, bf16[32,32,128]{2,1,0:T(8,128)(2,1)}, u32[]{:S(2)}) copy-start(bf16[32,32,128]{2,1,0:T(8,128)(2,1)} %param.6) | copy-start | bytes 786436
  11.3 17.3 %all-to-all-start = ((s32[16,2,32]{2,1,0:T(2,128)}), s32[16,2,32]{2,1,0:T(2,128)S(1)}, u32[]{:S(2)}, u32[]{:S(2)}) async-start(s32[16,2,32]{2,1,0:T(2,128)} %reshape.187), calls=%async_computation | async-start | bytes 32768 | tf_op jit(solution)/shard_map/all_to_all | solution.py:63
  33.1 163.8 %all-to-all-start.2 = ((bf16[16,2,32,32,128]{4,3,2,1,0:T(8,128)(2,1)}), bf16[16,2,32,32,128]{4,3,2,1,0:T(8,128)(2,1)}, u32[]{:S(2)}, u32[]{:S(2)}) async-start(bf16[16,2,32,32,128]{4,3,2,1,0:T(8,128)(2,1)} %bitcast.28), calls=%async_computation.2 | async-start | bytes 16777216 | tf_op jit(solution)/shard_map/all_to_all | solution.py:56
  226.3 9.1 %copy-start.1 = (s32[64]{0:T(128)S(1)}, s32[64]{0:T(128)}, u32[]{:S(2)}) copy-start(s32[64]{0:T(128)} %param.8) | copy-start | bytes 772
  226.3 9.1 %copy-start.2 = (bf16[64,128,128]{2,1,0:T(8,128)(2,1)S(1)}, bf16[64,128,128]{2,1,0:T(8,128)(2,1)}, u32[]{:S(2)}) copy-start(bf16[64,128,128]{2,1,0:T(8,128)(2,1)} %param.7) | copy-start | bytes 6291460
  312.0 43.7 %all-to-all-start.4 = ((f32[16,2,32]{2,1,0:T(2,128)}), f32[16,2,32]{2,1,0:T(2,128)S(1)}, u32[]{:S(2)}, u32[]{:S(2)}) async-start(f32[16,2,32]{2,1,0:T(2,128)} %reshape_reshape.11), calls=%async_computation.4 | async-start | bytes 32768 | tf_op jit(solution)/shard_map/all_to_all | solution.py:75
where the time goes:
time: 366 us; the launch traced here: 365 us
  waiting for transfers between devices  162 us (44%)
  local copies, waits for them, and re-layouts  78.7 us (22%)
  starting transfers between devices  51.6 us (14%)
  matrix products  39.1 us (11%)
  blocking collectives  30 us (8%)
    all_to_all x1, waiting for transfers between devices, shards(): lax.all_to_all(sent_rows, 'index', split_axis=0, concat_axis=0, tiled=True)  156 us
    dot_general x8, matrix products, score_group(): jnp.einsum('gtd,gpd->gtp', query_rows, block_rows, preferred_element_type...  39.1 us
    all_to_all x1, starting transfers between devices, shards(): lax.all_to_all(results.reshape(grid_shape), 'index', split_axis=0, concat...  37.5 us
    gather x8, local copies, waits for them, and re-layouts, score_group(): block_rows = passages[safe_ids]  24.5 us
    all_to_all x1, blocking collectives, shards(): lax.all_to_all(lax.all_to_all(sent_rows, 'index', split_axis=0, concat_ax...  20.5 us
    gather x1, local copies, waits for them, and re-layouts, shards(): sent_rows = queries[slot_query].reshape(grid_shape + queries.shape[1:])  9.91 us
    gather x8, local copies, waits for them, and re-layouts, score_group(): live = token_pos < lengths[safe_ids][:, None, None]  9.79 us
    all_to_all x1, local copies, waits for them, and re-layouts, shards(): lax.all_to_all(lax.all_to_all(sent_rows, 'index', split_axis=0, concat_ax...  9.1 us
  transfers between devices with their start and end apart: 3, of which 2 were waited for; matrix products, arithmetic and copies ran while one was open for 3% of the time, Pallas kernels for 0%

commit v1 on v0

v1 whole, which is shorter than its diff:
```python
import functools

import jax
import jax.numpy as jnp
from jax import lax
from jax.experimental import pallas as pl
from jax.experimental.pallas import tpu as pltpu
from jax.sharding import PartitionSpec as P

MESH = pl.DeviceIdType.MESH
LANES = 128
SUB = 8


def maxsim_kernel(
    n_index,
    n_query,
    q_hbm,
    p_hbm,
    len_ref,
    cand_ref,
    out_ref,
    q_buf,
    p_buf,
    qt_buf,
    best,
    sent,
    table,
    wide,
    q_sem,
    p_sem,
    q_send,
    q_recv,
    s_send,
    s_recv,
):
    me_i = lax.axis_index("index")
    me_q = lax.axis_index("query")
    n_dev = n_index * n_query
    my_slot = me_i * n_query + me_q
    groups, rows, dim = p_buf.shape
    blk_local = len_ref.shape[0]
    per_group = blk_local // groups
    tokens = rows // per_group
    q_rows = q_buf.shape[1]
    halves = sent.shape[1]
    part = q_rows // halves
    half = part // 2
    q_tok = half // SUB
    cand_local = cand_ref.shape[1]

    q_in = pltpu.make_async_copy(q_hbm, q_buf.at[0], q_sem)
    q_in.start()

    def p_copy(g):
        return pltpu.make_async_copy(p_hbm.at[g], p_buf.at[g], p_sem.at[g])

    for g in range(groups):
        p_copy(g).start()

    barrier = pltpu.get_barrier_semaphore()

    def greet(j, carry):
        other = lax.rem(my_slot + j, n_dev)
        pl.semaphore_signal(
            barrier,
            inc=1,
            device_id=(other // n_query, lax.rem(other, n_query)),
            device_id_type=MESH,
        )
        return carry

    lax.fori_loop(1, n_dev, greet, 0)

    token_pos = lax.broadcasted_iota(jnp.int32, (tokens, dim), 0)
    lane_q = lax.broadcasted_iota(jnp.int32, (SUB, half), 1) // q_tok
    row_q = lax.broadcasted_iota(jnp.int32, (SUB, half), 0)
    mean_w = jnp.where(lane_q == row_q, 1.0 / q_tok, 0.0).astype(jnp.bfloat16)

    def score_pass(k, m, first):
        qt_buf[...] = q_buf[k, pl.ds(m * part, part), :].T

        def group_step(g, carry):
            if first:
                p_copy(g).wait()
                for b in range(per_group):
                    block = p_buf[g, pl.ds(b * tokens, tokens), :].astype(jnp.float32)
                    live = token_pos < len_ref[g * per_group + b]
                    block = jnp.where(live, block, block[0:1, :])
                    p_buf[g, pl.ds(b * tokens, tokens), :] = block.astype(jnp.bfloat16)
            similar = jnp.dot(p_buf[g], qt_buf[...], preferred_element_type=jnp.float32)
            top = jnp.max(similar.reshape(per_group, tokens, part), axis=1)
            best[pl.ds(pl.multiple_of(g * per_group, per_group), per_group), :] = top[:, :half]
            best[
                pl.ds(pl.multiple_of(blk_local + g * per_group, per_group), per_group), :
            ] = top[:, half:]
            return carry

        lax.fori_loop(0, groups, group_step, 0)
        all_best = best[...]
        high = all_best.astype(jnp.bfloat16)
        low = (all_best - high.astype(jnp.float32)).astype(jnp.bfloat16)
        dims = (((1,), (1,)), ((), ()))
        sent[k, m] = lax.dot_general(
            mean_w, high, dims, preferred_element_type=jnp.float32
        ) + lax.dot_general(mean_w, low, dims, preferred_element_type=jnp.float32)

    def send_scores(k, m, own):
        to_q = lax.rem(me_q + k, n_query)

        def send(j, carry):
            pltpu.make_async_remote_copy(
                src_ref=sent.at[k, m],
                dst_ref=table.at[my_slot, m],
                send_sem=s_send,
                recv_sem=s_recv,
                device_id=(lax.rem(me_i + j, n_index), to_q),
                device_id_type=MESH,
            ).start()
            return carry

        lax.fori_loop(1 if own else 0, n_index, send, 0)
        if own:
            pltpu.make_async_copy(sent.at[k, m], table.at[my_slot, m], s_recv).start()

    def q_copy(k):
        return pltpu.make_async_remote_copy(
            src_ref=q_buf.at[0],
            dst_ref=q_buf.at[k],
            send_sem=q_send.at[k],
            recv_sem=q_recv.at[k],
            device_id=(me_i, lax.rem(me_q + n_query - k, n_query)),
            device_id_type=MESH,
        )

    q_in.wait()
    score_pass(0, 0, True)
    pl.semaphore_wait(barrier, n_dev - 1)
    for k in range(1, n_query):
        q_copy(k).start()
    send_scores(0, 0, True)
    for m in range(1, halves):
        score_pass(0, m, False)
        send_scores(0, m, True)

    def other_queries(k, carry):
        q_copy(k).wait_recv()
        for m in range(halves):
            score_pass(k, m, False)
            send_scores(k, m, False)
        return carry

    lax.fori_loop(1, n_query, other_queries, 0)

    wide[...] = jnp.zeros_like(wide)
    wide[:, :cand_local] = cand_ref[...]
    pltpu.make_async_copy(table, table, s_recv).wait()

    q_groups = cand_ref.shape[0] // SUB
    ids = [wide[pl.ds(g * SUB, SUB), :] for g in range(q_groups)]
    owners = [v // blk_local for v in ids]
    lanes = [
        v - o * blk_local + (g % 2) * blk_local for g, (v, o) in enumerate(zip(ids, owners))
    ]

    def pick(o, found):
        here = [table[o, m] for m in range(halves)]
        return tuple(
            jnp.where(
                owners[g] == o,
                jnp.take_along_axis(here[g // 2], lanes[g], axis=1),
                found[g],
            )
            for g in range(q_groups)
        )

    found = lax.fori_loop(
        0, n_dev, pick, tuple(jnp.zeros((SUB, LANES), jnp.float32) for _ in ids), unroll=8
    )
    for g in range(q_groups):
        out_ref[pl.ds(g * SUB, SUB), :] = found[g][:, :cand_local]

    pltpu.make_async_copy(
        table.at[pl.ds(0, n_dev - 1)], table.at[pl.ds(0, n_dev - 1)], s_send
    ).wait()
    for k in range(1, n_query):
        q_copy(k).wait_send()


def shards(n_index, n_query, queries, passages, lengths, candidates):
    q_local, q_tok, dim = queries.shape
    blk_local, tokens, _ = passages.shape
    per_group = SUB
    groups = blk_local // per_group
    q_rows = q_local * q_tok
    part = 2 * SUB * q_tok
    halves = q_rows // part
    n_dev = n_index * n_query
    flops = 2 * n_query * q_rows * blk_local * tokens * dim
    any_spec = pl.BlockSpec(memory_space=pl.ANY)
    vmem = pl.BlockSpec(memory_space=pltpu.VMEM)
    return pl.pallas_call(
        functools.partial(maxsim_kernel, n_index, n_query),
        out_shape=jax.ShapeDtypeStruct(candidates.shape, jnp.float32),
        in_specs=[any_spec, any_spec, pl.BlockSpec(memory_space=pltpu.SMEM), vmem],
        out_specs=vmem,
        scratch_shapes=[
            pltpu.VMEM((n_query, q_rows, dim), jnp.bfloat16),
            pltpu.VMEM((groups, per_group * tokens, dim), jnp.bfloat16),
            pltpu.VMEM((dim, part), jnp.bfloat16),
            pltpu.VMEM((2 * blk_local, part // 2), jnp.float32),
            pltpu.VMEM((n_query, halves, SUB, LANES), jnp.float32),
            pltpu.VMEM((n_dev, halves, SUB, LANES), jnp.float32),
            pltpu.VMEM((q_local, LANES), jnp.int32),
            pltpu.SemaphoreType.DMA,
            pltpu.SemaphoreType.DMA((groups,)),
            pltpu.SemaphoreType.DMA((n_query,)),
            pltpu.SemaphoreType.DMA((n_query,)),
            pltpu.SemaphoreType.DMA,
            pltpu.SemaphoreType.DMA,
        ],
        compiler_params=pltpu.CompilerParams(
            collective_id=0, has_side_effects=True, vmem_limit_bytes=40 * 1024 * 1024
        ),
        cost_estimate=pl.CostEstimate(
            flops=flops, bytes_accessed=passages.size * 2, transcendentals=0
        ),
        name="maxsim",
    )(
        queries.reshape(q_rows, dim),
        passages.reshape(groups, per_group * tokens, dim),
        lengths,
        candidates,
    )


def solution(mesh):
    in_specs = (
        P("query", None, None),
        P(("index", "query"), None, None),
        P(("index", "query")),
        P("query", "index"),
    )
    body = functools.partial(shards, mesh.shape["index"], mesh.shape["query"])
    return jax.shard_map(
        body, mesh=mesh, in_specs=in_specs, out_specs=P("query", "index"), check_vma=False
    )
```

time: 366 us -> 29.6 us (0.08)
  waiting for transfers between devices: 162 us -> 0 us
  local copies, waits for them, and re-layouts: 78.7 us -> 4.64 us
  starting transfers between devices: 51.6 us -> 0 us
  matrix products: 39.1 us -> 0 us
  blocking collectives: 30 us -> 0 us
  Pallas kernels: 0 us -> 24.8 us
    all_to_all x3 -> x0, waiting for transfers between devices: 162 us -> none  [the longest x1 156 us: shards(): lax.all_to_all(sent_rows, 'index', split_axis=0, concat_axis=0, tiled=True)]
    gather x19 -> x0, local copies, waits for them, and re-layouts: 53.3 us -> none  [the longest x8 24.5 us: score_group(): block_rows = passages[safe_ids]]
    all_to_all x3 -> x0, starting transfers between devices: 51.6 us -> none  [the longest x1 37.5 us: shards(): lax.all_to_all(results.reshape(grid_shape), 'index', split_axis=0, concat...]
    dot_general x8 -> x0, matrix products: 39.1 us -> none  [score_group(): jnp.einsum('gtd,gpd->gtp', query_rows, block_rows, preferred_element_type...]
    all_to_all x3 -> x0, blocking collectives: 30 us -> none  [the longest x1 20.5 us: shards(): lax.all_to_all(lax.all_to_all(sent_rows, 'index', split_axis=0, concat_ax...]
    pallas_call x0 -> x1, Pallas kernels: none -> 24.8 us  [shards(): pl.pallas_call(functools.partial(maxsim_kernel, n_index, n_query), out_sh...]
    all_to_all x8 -> x0, local copies, waits for them, and re-layouts: 19.1 us -> none  [the longest x1 9.1 us: shards(): lax.all_to_all(lax.all_to_all(sent_rows, 'index', split_axis=0, concat_ax...]
  transfers between devices with their start and end apart: 3 -> 0, of which waited for: 2 -> 0; matrix products, arithmetic and copies ran while one was open for 3% -> 0% of each run, Pallas kernels for 0% -> 0%
where the time goes in v1:
time: 29.6 us; the launch traced here: 29.4 us
  Pallas kernels  24.8 us (84%)
  local copies, waits for them, and re-layouts  4.64 us (16%)
    pallas_call x1, Pallas kernels, shards(): pl.pallas_call(functools.partial(maxsim_kernel, n_index, n_query), out_sh...  24.8 us
    unnamed x7, local copies, waits for them, and re-layouts  3.97 us
    pallas_call x1, local copies, waits for them, and re-layouts, shards(): pl.pallas_call(functools.partial(maxsim_kernel, n_index, n_query), out_sh...  0.67 us

profile of v1, /device:TPU:1, one launch (start us, length us, event | category | flops | bytes accessed | tf_op | source)
XLA Modules:
  0.0 29.4 jit_solution(17935911907291121739)
XLA Ops:
  0.0 0.8 %copy.5.cand_ref = s32[32,16]{1,0:T(8,128)S(1)} copy(s32[32,16]{0,1:T(8,128)} %param.7) | data formatting | bytes 4096 | tf_op args[3]
  0.8 0.0 copy-start
  0.8 1.6 %copy-done = bf16[64,128,128]{2,1,0:T(8,128)(2,1)S(1)} copy-done((bf16[64,128,128]{2,1,0:T(8,128)(2,1)S(1)}, bf16[64,128,128]{2,1,0:T(8,128)(2,1)}, u32[]{:S(2)}) %copy-start) | copy-done | bytes 2097176
  2.4 0.0 copy-start.1
  2.4 0.9 %copy-done.1 = bf16[32,32,128]{2,1,0:T(8,128)(2,1)S(1)} copy-done((bf16[32,32,128]{2,1,0:T(8,128)(2,1)S(1)}, bf16[32,32,128]{2,1,0:T(8,128)(2,1)}, u32[]{:S(2)}) %copy-start.1) | copy-done | bytes 262168
  3.3 0.0 copy-start.2
  3.3 0.7 %copy-done.2 = s32[64]{0:T(128)S(1)} copy-done((s32[64]{0:T(128)S(1)}, s32[64]{0:T(128)}, u32[]{:S(2)}) %copy-start.2) | copy-done | bytes 280
  4.0 24.8 %maxsim.1 = f32[32,16]{1,0:T(8,128)S(1)} custom-call(bf16[1024,128]{1,0:T(8,128)(2,1)S(1)} %bitcast.3, bf16[8,1024,128]{2,1,0:T(8,128)(2,1)S(1)} %bitcast.2, s32[64]{0:T(128)S(1)} %copy-done.2, s32[32,16]{1,0:T(8,128)S(1)} %copy.5.cand_ref), custom_call_target="tpu_custom_call" | custom-call | flops 4294967296 | bytes 2097152 | tf_op jit(solution)/shard_map/maxsim/pallas_call | solution.py:202
  28.8 0.7 %copy.6 = f32[32,16]{0,1:T(8,128)} copy(f32[32,16]{1,0:T(8,128)S(1)} %maxsim.1) | data formatting | bytes 4096 | tf_op jit(solution)/shard_map/maxsim/pallas_call | solution.py:202
Async XLA Ops:
  0.8 1.6 %copy-start = (bf16[64,128,128]{2,1,0:T(8,128)(2,1)S(1)}, bf16[64,128,128]{2,1,0:T(8,128)(2,1)}, u32[]{:S(2)}) copy-start(bf16[64,128,128]{2,1,0:T(8,128)(2,1)} %param.5) | copy-start | bytes 6291460
  2.4 0.9 %copy-start.1 = (bf16[32,32,128]{2,1,0:T(8,128)(2,1)S(1)}, bf16[32,32,128]{2,1,0:T(8,128)(2,1)}, u32[]{:S(2)}) copy-start(bf16[32,32,128]{2,1,0:T(8,128)(2,1)} %param.4) | copy-start | bytes 786436
  3.3 0.7 %copy-start.2 = (s32[64]{0:T(128)S(1)}, s32[64]{0:T(128)}, u32[]{:S(2)}) copy-start(s32[64]{0:T(128)} %len_ref.1) | copy-start | bytes 772

commit v2 on v1

--- a/solution.py
+++ b/solution.py
@@ -17,9 +17,11 @@
     n_query,
     q_hbm,
     p_hbm,
+    len_hbm,
+    cand_hbm,
+    out_ref,
     len_ref,
     cand_ref,
-    out_ref,
     q_buf,
     p_buf,
     qt_buf,
@@ -33,6 +35,8 @@
     q_recv,
     s_send,
     s_recv,
+    len_sem,
+    cand_sem,
 ):
     me_i = lax.axis_index("index")
     me_q = lax.axis_index("query")
@@ -47,16 +51,20 @@
     part = q_rows // halves
     half = part // 2
     q_tok = half // SUB
-    cand_local = cand_ref.shape[1]
+    cand_local = cand_ref.shape[0]
 
     q_in = pltpu.make_async_copy(q_hbm, q_buf.at[0], q_sem)
     q_in.start()
+    len_in = pltpu.make_async_copy(len_hbm, len_ref, len_sem)
+    len_in.start()
 
     def p_copy(g):
         return pltpu.make_async_copy(p_hbm.at[g], p_buf.at[g], p_sem.at[g])
 
     for g in range(groups):
         p_copy(g).start()
+    cand_in = pltpu.make_async_copy(cand_hbm, cand_ref, cand_sem)
+    cand_in.start()
 
     barrier = pltpu.get_barrier_semaphore()
 
@@ -83,12 +91,16 @@
         def group_step(g, carry):
             if first:
                 p_copy(g).wait()
+                blocks = []
                 for b in range(per_group):
                     block = p_buf[g, pl.ds(b * tokens, tokens), :].astype(jnp.float32)
                     live = token_pos < len_ref[g * per_group + b]
-                    block = jnp.where(live, block, block[0:1, :])
-                    p_buf[g, pl.ds(b * tokens, tokens), :] = block.astype(jnp.bfloat16)
-            similar = jnp.dot(p_buf[g], qt_buf[...], preferred_element_type=jnp.float32)
+                    blocks.append(jnp.where(live, block, block[0:1, :]).astype(jnp.bfloat16))
+                group_rows = jnp.concatenate(blocks, axis=0)
+                p_buf[g] = group_rows
+            else:
+                group_rows = p_buf[g]
+            similar = jnp.dot(group_rows, qt_buf[...], preferred_element_type=jnp.float32)
             top = jnp.max(similar.reshape(per_group, tokens, part), axis=1)
             best[pl.ds(pl.multiple_of(g * per_group, per_group), per_group), :] = top[:, :half]
             best[
@@ -96,7 +108,7 @@
             ] = top[:, half:]
             return carry
 
-        lax.fori_loop(0, groups, group_step, 0)
+        lax.fori_loop(0, groups, group_step, 0, unroll=2)
         all_best = best[...]
         high = all_best.astype(jnp.bfloat16)
         low = (all_best - high.astype(jnp.float32)).astype(jnp.bfloat16)
@@ -134,6 +146,7 @@
         )
 
     q_in.wait()
+    len_in.wait()
     score_pass(0, 0, True)
     pl.semaphore_wait(barrier, n_dev - 1)
     for k in range(1, n_query):
@@ -152,11 +165,12 @@
 
     lax.fori_loop(1, n_query, other_queries, 0)
 
+    cand_in.wait()
     wide[...] = jnp.zeros_like(wide)
-    wide[:, :cand_local] = cand_ref[...]
+    wide[:, :cand_local] = cand_ref[...].T
     pltpu.make_async_copy(table, table, s_recv).wait()
 
-    q_groups = cand_ref.shape[0] // SUB
+    q_groups = cand_ref.shape[1] // SUB
     ids = [wide[pl.ds(g * SUB, SUB), :] for g in range(q_groups)]
     owners = [v // blk_local for v in ids]
     lanes = [
@@ -177,8 +191,8 @@
     found = lax.fori_loop(
         0, n_dev, pick, tuple(jnp.zeros((SUB, LANES), jnp.float32) for _ in ids), unroll=8
     )
-    for g in range(q_groups):
-        out_ref[pl.ds(g * SUB, SUB), :] = found[g][:, :cand_local]
+    scores = jnp.concatenate([v[:, :cand_local] for v in found], axis=0)
+    out_ref[...] = scores.T
 
     pltpu.make_async_copy(
         table.at[pl.ds(0, n_dev - 1)], table.at[pl.ds(0, n_dev - 1)], s_send
@@ -197,14 +211,16 @@
     halves = q_rows // part
     n_dev = n_index * n_query
     flops = 2 * n_query * q_rows * blk_local * tokens * dim
-    any_spec = pl.BlockSpec(memory_space=pl.ANY)
+    hbm = pl.BlockSpec(memory_space=pltpu.HBM)
     vmem = pl.BlockSpec(memory_space=pltpu.VMEM)
     return pl.pallas_call(
         functools.partial(maxsim_kernel, n_index, n_query),
-        out_shape=jax.ShapeDtypeStruct(candidates.shape, jnp.float32),
-        in_specs=[any_spec, any_spec, pl.BlockSpec(memory_space=pltpu.SMEM), vmem],
+        out_shape=jax.ShapeDtypeStruct(candidates.shape[::-1], jnp.float32),
+        in_specs=[hbm, hbm, hbm, hbm],
         out_specs=vmem,
         scratch_shapes=[
+            pltpu.SMEM(lengths.shape, jnp.int32),
+            pltpu.VMEM(candidates.shape[::-1], jnp.int32),
             pltpu.VMEM((n_query, q_rows, dim), jnp.bfloat16),
             pltpu.VMEM((groups, per_group * tokens, dim), jnp.bfloat16),
             pltpu.VMEM((dim, part), jnp.bfloat16),
@@ -218,9 +234,11 @@
             pltpu.SemaphoreType.DMA((n_query,)),
             pltpu.SemaphoreType.DMA,
             pltpu.SemaphoreType.DMA,
+            pltpu.SemaphoreType.DMA,
+            pltpu.SemaphoreType.DMA,
         ],
         compiler_params=pltpu.CompilerParams(
-            collective_id=0, has_side_effects=True, vmem_limit_bytes=40 * 1024 * 1024
+            collective_id=0, has_side_effects=True, vmem_limit_bytes=60 * 1024 * 1024
         ),
         cost_estimate=pl.CostEstimate(
             flops=flops, bytes_accessed=passages.size * 2, transcendentals=0
@@ -230,8 +248,8 @@
         queries.reshape(q_rows, dim),
         passages.reshape(groups, per_group * tokens, dim),
         lengths,
-        candidates,
-    )
+        candidates.T,
+    ).T
 
 
 def solution(mesh):

time: 29.6 us -> 25.4 us (0.86)
  local copies, waits for them, and re-layouts: 4.64 us -> 1.3 us
  Pallas kernels: 24.8 us -> 23.8 us
    unnamed x7 -> x1, local copies, waits for them, and re-layouts: 3.97 us -> 1.3 us
    pallas_call x1, Pallas kernels: 24.8 us -> 23.8 us  [shards(): pl.pallas_call(functools.partial(maxsim_kernel, n_index, n_query), out_sh...]
    pallas_call x1 -> x0, local copies, waits for them, and re-layouts: 0.67 us -> none  [shards(): pl.pallas_call(functools.partial(maxsim_kernel, n_index, n_query), out_sh...]
where the time goes in v2:
time: 25.4 us; the launch traced here: 25.1 us
  Pallas kernels  23.8 us (94%)
  local copies, waits for them, and re-layouts  1.3 us (5%)
    pallas_call x1, Pallas kernels, shards(): pl.pallas_call(functools.partial(maxsim_kernel, n_index, n_query), out_sh...  23.8 us
    unnamed x1, local copies, waits for them, and re-layouts  1.3 us

profile of v2, /device:TPU:1, one launch (start us, length us, event | category | flops | bytes accessed | tf_op | source)
XLA Modules:
  0.0 25.1 jit_solution(15448163192295686982)
XLA Ops:
  0.0 23.8 %maxsim.1 = f32[16,32]{1,0:T(8,128)} custom-call(bf16[1024,128]{1,0:T(8,128)(2,1)} %bitcast.6, bf16[8,1024,128]{2,1,0:T(8,128)(2,1)} %bitcast.5, s32[64]{0:T(128)} %len_hbm.1, s32[16,32]{1,0:T(8,128)} %bitcast.7), custom_call_target="tpu_custom_call" | custom-call | flops 4294967296 | bytes 2097152 | tf_op jit(solution)/shard_map/maxsim/pallas_call | solution.py:216
  23.9 1.3 %copy.6 = f32[32,16]{0,1:T(8,128)} copy(f32[32,16]{0,1:T(8,128)} %bitcast.4) | data formatting | bytes 4096

commit v3 on v2

--- a/solution.py
+++ b/solution.py
@@ -86,7 +86,7 @@
     mean_w = jnp.where(lane_q == row_q, 1.0 / q_tok, 0.0).astype(jnp.bfloat16)
 
     def score_pass(k, m, first):
-        qt_buf[...] = q_buf[k, pl.ds(m * part, part), :].T
+        qt_buf[...] = q_buf[k, pl.ds(pl.multiple_of(m * part, part), part), :].T
 
         def group_step(g, carry):
             if first:
@@ -108,7 +108,7 @@
             ] = top[:, half:]
             return carry
 
-        lax.fori_loop(0, groups, group_step, 0, unroll=2)
+        lax.fori_loop(0, groups, group_step, 0, unroll=4)
         all_best = best[...]
         high = all_best.astype(jnp.bfloat16)
         low = (all_best - high.astype(jnp.float32)).astype(jnp.bfloat16)
@@ -117,8 +117,9 @@
             mean_w, high, dims, preferred_element_type=jnp.float32
         ) + lax.dot_general(mean_w, low, dims, preferred_element_type=jnp.float32)
 
-    def send_scores(k, m, own):
+    def send_scores(k, m):
         to_q = lax.rem(me_q + k, n_query)
+        own = jnp.where(k == 0, 1, 0)
 
         def send(j, carry):
             pltpu.make_async_remote_copy(
@@ -131,8 +132,10 @@
             ).start()
             return carry
 
-        lax.fori_loop(1 if own else 0, n_index, send, 0)
-        if own:
+        lax.fori_loop(own, n_index, send, 0)
+
+        @pl.when(own == 1)
+        def _():
             pltpu.make_async_copy(sent.at[k, m], table.at[my_slot, m], s_recv).start()
 
     def q_copy(k):
@@ -151,19 +154,21 @@
     pl.semaphore_wait(barrier, n_dev - 1)
     for k in range(1, n_query):
         q_copy(k).start()
-    send_scores(0, 0, True)
-    for m in range(1, halves):
-        score_pass(0, m, False)
-        send_scores(0, m, True)
-
-    def other_queries(k, carry):
-        q_copy(k).wait_recv()
-        for m in range(halves):
-            score_pass(k, m, False)
-            send_scores(k, m, False)
+    send_scores(0, 0)
+
+    def later_pass(step, carry):
+        k = step // halves
+        m = lax.rem(step, halves)
+
+        @pl.when((k > 0) & (m == 0))
+        def _():
+            q_copy(k).wait_recv()
+
+        score_pass(k, m, False)
+        send_scores(k, m)
         return carry
 
-    lax.fori_loop(1, n_query, other_queries, 0)
+    lax.fori_loop(1, n_query * halves, later_pass, 0)
 
     cand_in.wait()
     wide[...] = jnp.zeros_like(wide)

time: 25.4 us -> 24.5 us (0.965)
  Pallas kernels: 23.8 us -> 23 us
    pallas_call x1, Pallas kernels: 23.8 us -> 23 us  [shards(): pl.pallas_call(functools.partial(maxsim_kernel, n_index, n_query), out_sh...]
where the time goes in v3:
time: 24.5 us; the launch traced here: 24.3 us
  Pallas kernels  23 us (94%)
  local copies, waits for them, and re-layouts  1.3 us (5%)
    pallas_call x1, Pallas kernels, shards(): pl.pallas_call(functools.partial(maxsim_kernel, n_index, n_query), out_sh...  23 us
    unnamed x1, local copies, waits for them, and re-layouts  1.3 us

profile of v3, /device:TPU:1, one launch (start us, length us, event | category | flops | bytes accessed | tf_op | source)
XLA Modules:
  0.0 24.3 jit_solution(6651875887587743422)
XLA Ops:
  0.0 23.0 %maxsim.1 = f32[16,32]{1,0:T(8,128)} custom-call(bf16[1024,128]{1,0:T(8,128)(2,1)} %bitcast.6, bf16[8,1024,128]{2,1,0:T(8,128)(2,1)} %bitcast.5, s32[64]{0:T(128)} %len_hbm.1, s32[16,32]{1,0:T(8,128)} %bitcast.7), custom_call_target="tpu_custom_call" | custom-call | flops 4294967296 | bytes 2097152 | tf_op jit(solution)/shard_map/maxsim/pallas_call | solution.py:221
  23.0 1.3 %copy.6 = f32[32,16]{0,1:T(8,128)} copy(f32[32,16]{0,1:T(8,128)} %bitcast.4) | data formatting | bytes 4096

commit v4 on v3

--- a/solution.py
+++ b/solution.py
@@ -108,7 +108,7 @@
             ] = top[:, half:]
             return carry
 
-        lax.fori_loop(0, groups, group_step, 0, unroll=4)
+        lax.fori_loop(0, groups, group_step, 0, unroll=4 if first else 8)
         all_best = best[...]
         high = all_best.astype(jnp.bfloat16)
         low = (all_best - high.astype(jnp.float32)).astype(jnp.bfloat16)
@@ -220,7 +220,7 @@
     vmem = pl.BlockSpec(memory_space=pltpu.VMEM)
     return pl.pallas_call(
         functools.partial(maxsim_kernel, n_index, n_query),
-        out_shape=jax.ShapeDtypeStruct(candidates.shape[::-1], jnp.float32),
+        out_shape=pltpu.VMEM(candidates.shape[::-1], jnp.float32),
         in_specs=[hbm, hbm, hbm, hbm],
         out_specs=vmem,
         scratch_shapes=[

time: 24.5 us -> 22.5 us (0.918)
  Pallas kernels: 23 us -> 21.7 us
  local copies, waits for them, and re-layouts: 1.3 us -> 0.6 us
    pallas_call x1, Pallas kernels: 23 us -> 21.7 us  [shards(): pl.pallas_call(functools.partial(maxsim_kernel, n_index, n_query), out_sh...]
    unnamed x1, local copies, waits for them, and re-layouts: 1.3 us -> 0.6 us
where the time goes in v4:
time: 22.5 us; the launch traced here: 22.4 us
  Pallas kernels  21.7 us (96%)
  local copies, waits for them, and re-layouts  0.6 us (3%)
    pallas_call x1, Pallas kernels, shards(): pl.pallas_call(functools.partial(maxsim_kernel, n_index, n_query), out_sh...  21.7 us
    unnamed x1, local copies, waits for them, and re-layouts  0.6 us

profile of v4, /device:TPU:1, one launch (start us, length us, event | category | flops | bytes accessed | tf_op | source)
XLA Modules:
  0.0 22.4 jit_solution(7924322359617196376)
XLA Ops:
  0.0 21.7 %maxsim.1 = f32[16,32]{1,0:T(8,128)S(1)} custom-call(bf16[1024,128]{1,0:T(8,128)(2,1)} %bitcast.6, bf16[8,1024,128]{2,1,0:T(8,128)(2,1)} %bitcast.5, s32[64]{0:T(128)} %len_hbm.1, s32[16,32]{1,0:T(8,128)} %bitcast.7), custom_call_target="tpu_custom_call" | custom-call | flops 4294967296 | bytes 2097152 | tf_op jit(solution)/shard_map/maxsim/pallas_call | solution.py:221
  21.8 0.6 %copy.6 = f32[32,16]{0,1:T(8,128)} copy(f32[32,16]{0,1:T(8,128)S(1)} %bitcast.4) | data formatting | bytes 4096

commit v5 on v4

--- a/solution.py
+++ b/solution.py
@@ -85,10 +85,9 @@
     row_q = lax.broadcasted_iota(jnp.int32, (SUB, half), 0)
     mean_w = jnp.where(lane_q == row_q, 1.0 / q_tok, 0.0).astype(jnp.bfloat16)
 
-    def score_pass(k, m, first):
+    def score_pass(k, m, side, first, between):
         qt_buf[...] = q_buf[k, pl.ds(pl.multiple_of(m * part, part), part), :].T
-
-        def group_step(g, carry):
+        for g in range(groups):
             if first:
                 p_copy(g).wait()
                 blocks = []
@@ -102,14 +101,13 @@
                 group_rows = p_buf[g]
             similar = jnp.dot(group_rows, qt_buf[...], preferred_element_type=jnp.float32)
             top = jnp.max(similar.reshape(per_group, tokens, part), axis=1)
-            best[pl.ds(pl.multiple_of(g * per_group, per_group), per_group), :] = top[:, :half]
-            best[
-                pl.ds(pl.multiple_of(blk_local + g * per_group, per_group), per_group), :
-            ] = top[:, half:]
-            return carry
-
-        lax.fori_loop(0, groups, group_step, 0, unroll=4 if first else 8)
-        all_best = best[...]
+            best[side, pl.ds(g * per_group, per_group), :] = top[:, :half]
+            best[side, pl.ds(blk_local + g * per_group, per_group), :] = top[:, half:]
+            if g == 0:
+                between()
+
+    def mean_scores(k, m, side):
+        all_best = best[side]
         high = all_best.astype(jnp.bfloat16)
         low = (all_best - high.astype(jnp.float32)).astype(jnp.bfloat16)
         dims = (((1,), (1,)), ((), ()))
@@ -117,24 +115,26 @@
             mean_w, high, dims, preferred_element_type=jnp.float32
         ) + lax.dot_general(mean_w, low, dims, preferred_element_type=jnp.float32)
 
-    def send_scores(k, m):
-        to_q = lax.rem(me_q + k, n_query)
-        own = jnp.where(k == 0, 1, 0)
-
-        def send(j, carry):
-            pltpu.make_async_remote_copy(
-                src_ref=sent.at[k, m],
-                dst_ref=table.at[my_slot, m],
-                send_sem=s_send,
-                recv_sem=s_recv,
-                device_id=(lax.rem(me_i + j, n_index), to_q),
-                device_id_type=MESH,
-            ).start()
-            return carry
-
-        lax.fori_loop(own, n_index, send, 0)
-
-        @pl.when(own == 1)
+    def send_one(k, m, j):
+        pltpu.make_async_remote_copy(
+            src_ref=sent.at[k, m],
+            dst_ref=table.at[my_slot, m],
+            send_sem=s_send,
+            recv_sem=s_recv,
+            device_id=(lax.rem(me_i + j, n_index), lax.rem(me_q + k, n_query)),
+            device_id_type=MESH,
+        ).start()
+
+    def send_rest(k, m):
+        for j in range(1, n_index):
+            send_one(k, m, j)
+
+    def send_near(k, m):
+        @pl.when(k > 0)
+        def _():
+            send_one(k, m, 0)
+
+        @pl.when(k == 0)
         def _():
             pltpu.make_async_copy(sent.at[k, m], table.at[my_slot, m], s_recv).start()
 
@@ -150,37 +150,45 @@
 
     q_in.wait()
     len_in.wait()
-    score_pass(0, 0, True)
+    score_pass(0, 0, 0, True, lambda: None)
     pl.semaphore_wait(barrier, n_dev - 1)
     for k in range(1, n_query):
         q_copy(k).start()
-    send_scores(0, 0)
 
     def later_pass(step, carry):
         k = step // halves
         m = lax.rem(step, halves)
+        old = step - 1
+        old_k = old // halves
+        old_m = lax.rem(old, halves)
 
         @pl.when((k > 0) & (m == 0))
         def _():
             q_copy(k).wait_recv()
 
-        score_pass(k, m, False)
-        send_scores(k, m)
+        mean_scores(old_k, old_m, lax.rem(old, 2))
+        score_pass(k, m, lax.rem(step, 2), False, lambda: send_rest(old_k, old_m))
+        send_near(old_k, old_m)
         return carry
 
-    lax.fori_loop(1, n_query * halves, later_pass, 0)
+    passes = n_query * halves
+    lax.fori_loop(1, passes, later_pass, 0)
+    last_k, last_m = n_query - 1, halves - 1
+    mean_scores(last_k, last_m, (passes - 1) % 2)
+    send_rest(last_k, last_m)
+    send_near(last_k, last_m)
 
     cand_in.wait()
     wide[...] = jnp.zeros_like(wide)
     wide[:, :cand_local] = cand_ref[...].T
-    pltpu.make_async_copy(table, table, s_recv).wait()
-
     q_groups = cand_ref.shape[1] // SUB
     ids = [wide[pl.ds(g * SUB, SUB), :] for g in range(q_groups)]
     owners = [v // blk_local for v in ids]
     lanes = [
         v - o * blk_local + (g % 2) * blk_local for g, (v, o) in enumerate(zip(ids, owners))
     ]
+
+    pltpu.make_async_copy(table, table, s_recv).wait()
 
     def pick(o, found):
         here = [table[o, m] for m in range(halves)]
@@ -229,7 +237,7 @@
             pltpu.VMEM((n_query, q_rows, dim), jnp.bfloat16),
             pltpu.VMEM((groups, per_group * tokens, dim), jnp.bfloat16),
             pltpu.VMEM((dim, part), jnp.bfloat16),
-            pltpu.VMEM((2 * blk_local, part // 2), jnp.float32),
+            pltpu.VMEM((2, 2 * blk_local, part // 2), jnp.float32),
             pltpu.VMEM((n_query, halves, SUB, LANES), jnp.float32),
             pltpu.VMEM((n_dev, halves, SUB, LANES), jnp.float32),
             pltpu.VMEM((q_local, LANES), jnp.int32),

time: 22.5 us -> 22.5 us (level)
  no operation moved by 1% of the time
where the time goes in v5:
time: 22.5 us; the launch traced here: 22.3 us
  Pallas kernels  21.7 us (96%)
  local copies, waits for them, and re-layouts  0.6 us (3%)
    pallas_call x1, Pallas kernels, shards(): pl.pallas_call(functools.partial(maxsim_kernel, n_index, n_query), out_sh...  21.7 us
    unnamed x1, local copies, waits for them, and re-layouts  0.6 us

profile of v5, /device:TPU:1, one launch (start us, length us, event | category | flops | bytes accessed | tf_op | source)
XLA Modules:
  0.0 22.3 jit_solution(5245291749815353637)
XLA Ops:
  0.0 21.7 %maxsim.1 = f32[16,32]{1,0:T(8,128)S(1)} custom-call(bf16[1024,128]{1,0:T(8,128)(2,1)} %bitcast.6, bf16[8,1024,128]{2,1,0:T(8,128)(2,1)} %bitcast.5, s32[64]{0:T(128)} %len_hbm.1, s32[16,32]{1,0:T(8,128)} %bitcast.7), custom_call_target="tpu_custom_call" | custom-call | flops 4294967296 | bytes 2097152 | tf_op jit(solution)/shard_map/maxsim/pallas_call | solution.py:229
  21.7 0.6 %copy.6 = f32[32,16]{0,1:T(8,128)} copy(f32[32,16]{0,1:T(8,128)S(1)} %bitcast.4) | data formatting | bytes 4096

commit v6 on v5

--- a/solution.py
+++ b/solution.py
@@ -85,6 +85,28 @@
     row_q = lax.broadcasted_iota(jnp.int32, (SUB, half), 0)
     mean_w = jnp.where(lane_q == row_q, 1.0 / q_tok, 0.0).astype(jnp.bfloat16)
 
+    def fold_rows(tops):
+        row = lax.broadcasted_iota(jnp.int32, tops[0].shape, 0)
+        step = SUB // 2
+        while len(tops) > 1:
+            low = (row & step) == 0
+            count = len(tops) // 2
+            tops = [
+                jnp.maximum(
+                    jnp.where(low, tops[i], tops[i + count]),
+                    pltpu.roll(jnp.where(low, tops[i + count], tops[i]), step, axis=0)
+                    if step * 2 == SUB
+                    else jnp.where(
+                        low,
+                        pltpu.roll(tops[i], SUB - step, axis=0),
+                        pltpu.roll(tops[i + count], step, axis=0),
+                    ),
+                )
+                for i in range(count)
+            ]
+            step //= 2
+        return tops[0]
+
     def score_pass(k, m, side, first, between):
         qt_buf[...] = q_buf[k, pl.ds(pl.multiple_of(m * part, part), part), :].T
         for g in range(groups):
@@ -100,7 +122,9 @@
             else:
                 group_rows = p_buf[g]
             similar = jnp.dot(group_rows, qt_buf[...], preferred_element_type=jnp.float32)
-            top = jnp.max(similar.reshape(per_group, tokens, part), axis=1)
+            pieces = similar.reshape(per_group, tokens // SUB, SUB, part)
+            tops = [jnp.max(pieces[b], axis=0) for b in range(per_group)]
+            top = fold_rows(tops)
             best[side, pl.ds(g * per_group, per_group), :] = top[:, :half]
             best[side, pl.ds(blk_local + g * per_group, per_group), :] = top[:, half:]
             if g == 0:

time: 22.5 us -> 22.5 us (level)
  no operation moved by 1% of the time
where the time goes in v6:
time: 22.5 us; the launch traced here: 22.4 us
  Pallas kernels  21.7 us (96%)
  local copies, waits for them, and re-layouts  0.6 us (3%)
    pallas_call x1, Pallas kernels, shards(): pl.pallas_call(functools.partial(maxsim_kernel, n_index, n_query), out_sh...  21.7 us
    unnamed x1, local copies, waits for them, and re-layouts  0.6 us

profile of v6, /device:TPU:1, one launch (start us, length us, event | category | flops | bytes accessed | tf_op | source)
XLA Modules:
  0.0 22.4 jit_solution(4158329732527044611)
XLA Ops:
  0.0 21.7 %maxsim.1 = f32[16,32]{1,0:T(8,128)S(1)} custom-call(bf16[1024,128]{1,0:T(8,128)(2,1)} %bitcast.6, bf16[8,1024,128]{2,1,0:T(8,128)(2,1)} %bitcast.5, s32[64]{0:T(128)} %len_hbm.1, s32[16,32]{1,0:T(8,128)} %bitcast.7), custom_call_target="tpu_custom_call" | custom-call | flops 4294967296 | bytes 2097152 | tf_op jit(solution)/shard_map/maxsim/pallas_call | solution.py:253
  21.8 0.6 %copy.6 = f32[32,16]{0,1:T(8,128)} copy(f32[32,16]{0,1:T(8,128)S(1)} %bitcast.4) | data formatting | bytes 4096

commit v7 on v6

--- a/solution.py
+++ b/solution.py
@@ -121,12 +121,15 @@
                 p_buf[g] = group_rows
             else:
                 group_rows = p_buf[g]
-            similar = jnp.dot(group_rows, qt_buf[...], preferred_element_type=jnp.float32)
-            pieces = similar.reshape(per_group, tokens // SUB, SUB, part)
-            tops = [jnp.max(pieces[b], axis=0) for b in range(per_group)]
-            top = fold_rows(tops)
-            best[side, pl.ds(g * per_group, per_group), :] = top[:, :half]
-            best[side, pl.ds(blk_local + g * per_group, per_group), :] = top[:, half:]
+            for h in range(2):
+                similar = jnp.dot(
+                    group_rows,
+                    qt_buf[:, h * half : (h + 1) * half],
+                    preferred_element_type=jnp.float32,
+                )
+                pieces = similar.reshape(per_group, tokens // SUB, SUB, half)
+                tops = [jnp.max(pieces[b], axis=0) for b in range(per_group)]
+                best[side, pl.ds(h * blk_local + g * per_group, per_group), :] = fold_rows(tops)
             if g == 0:
                 between()
 

time: 22.5 us -> 22.5 us (level)
  no operation moved by 1% of the time
where the time goes in v7:
time: 22.5 us; the launch traced here: 22.4 us
  Pallas kernels  21.7 us (96%)
  local copies, waits for them, and re-layouts  0.6 us (3%)
    pallas_call x1, Pallas kernels, shards(): pl.pallas_call(functools.partial(maxsim_kernel, n_index, n_query), out_sh...  21.7 us
    unnamed x1, local copies, waits for them, and re-layouts  0.6 us

profile of v7, /device:TPU:1, one launch (start us, length us, event | category | flops | bytes accessed | tf_op | source)
XLA Modules:
  0.0 22.4 jit_solution(4158329732527044611)
XLA Ops:
  0.0 21.7 %maxsim.1 = f32[16,32]{1,0:T(8,128)S(1)} custom-call(bf16[1024,128]{1,0:T(8,128)(2,1)} %bitcast.6, bf16[8,1024,128]{2,1,0:T(8,128)(2,1)} %bitcast.5, s32[64]{0:T(128)} %len_hbm.1, s32[16,32]{1,0:T(8,128)} %bitcast.7), custom_call_target="tpu_custom_call" | custom-call | flops 4294967296 | bytes 2097152 | tf_op jit(solution)/shard_map/maxsim/pallas_call | solution.py:256
  21.8 0.6 %copy.6 = f32[32,16]{0,1:T(8,128)} copy(f32[32,16]{0,1:T(8,128)S(1)} %bitcast.4) | data formatting | bytes 4096
